TPU v7x, 512 devices: a whole 4x4x16 slice. The times are simulated.
512 devices in a mesh: gx: 64 (over x, z), gy: 8 (over y, core).
Axes of the slice: x: 4, y: 4, z: 16, core: 2. Of those that a mesh axis runs over, the one named last changes fastest.
Arguments:
- snapshot: bfloat16 [3, 512, 128, 1024], P(None, 'gx', 'gy'), may hold values from -6 to 6
- basis: bfloat16 [3, 64, 16, 128, 512], P(None, 'gx', 'gy'), may hold values from -3000 to 3000
- taps: bfloat16 [3, 17], replicated, may hold values from 0.099609375 to 1
Outputs:
- new_modes: bfloat16 [3, 64, 16, 128, 512], P(None, 'gx', 'gy')
- new_mode: float32 [3, 64, 16, 128], P(None, 'gx', 'gy')
- factor: float32 [513, 513], replicated
All inputs are finite; a program needn't handle non-finite values.
Results may differ from a plain program's by a relative error of at most 0.0012.
The roundings to bfloat16 on the way count: a program that leaves them out, or rounds other values in their place, can miss the bound.
Values sent between devices are 32-bit elements; how exact they have to be, the bound alone decides.
A program may use at most 64 MiB of HBM per device.

v0:
```python
import jax
import jax.numpy as jnp
from jax import lax
from jax.sharding import PartitionSpec as P

STRIDE = 8


def padded(block, sides, width, periodic):
    for axis, dim in sides:
        count = lax.axis_size(axis)
        forward = [(i, i + 1) for i in range(count - 1)]
        if periodic:
            forward.append((count - 1, 0))
        backward = [(target, source) for source, target in forward]
        low = lax.ppermute(
            lax.slice_in_dim(block, block.shape[dim] - width, None, axis=dim), axis, forward
        )
        high = lax.ppermute(lax.slice_in_dim(block, 0, width, axis=dim), axis, backward)
        block = jnp.concatenate([low, block, high], axis=dim)
    return block


def band(taps_row, length, out_len, shift, wrap):
    rows = jnp.arange(length, dtype=jnp.int32)[:, None]
    cols = jnp.arange(out_len, dtype=jnp.int32)[None, :]
    lag = rows - STRIDE * cols + shift
    if wrap:
        lag = lag % length
    hits = lag[:, :, None] == jnp.arange(2 * STRIDE + 1, dtype=jnp.int32)[None, None, :]
    return jnp.sum(jnp.where(hits, taps_row[None, None, :], jnp.zeros((), taps_row.dtype)), axis=-1)


def local(snapshot, basis, taps):
    comps, cells_x, cells_y, cells_z = snapshot.shape
    modes = basis.shape[-1]
    flat_rows = basis.reshape(-1, modes)
    total = flat_rows.shape[0] * lax.axis_size("gx") * lax.axis_size("gy")
    matrix_z = band(taps[2], cells_z, cells_z // STRIDE, STRIDE, True)
    along_z = jnp.dot(snapshot.reshape(-1, cells_z), matrix_z, preferred_element_type=jnp.float32)
    along_z = along_z.reshape(comps, cells_x, cells_y, cells_z // STRIDE)
    padded_y = padded(along_z, (("gy", 2),), STRIDE, False)
    matrix_y = band(taps[1], cells_y + 2 * STRIDE, cells_y // STRIDE, 0, False).astype(jnp.float32)
    along_y = jnp.einsum("cxyz,yf->cxfz", padded_y, matrix_y, precision=lax.Precision.HIGHEST)
    padded_x = padded(along_y, (("gx", 1),), STRIDE, True)
    matrix_x = band(taps[0], cells_x + 2 * STRIDE, cells_x // STRIDE, 0, False).astype(jnp.float32)
    along_x = jnp.einsum("cxyz,xf->cfyz", padded_x, matrix_x, precision=lax.Precision.HIGHEST)
    filtered = along_x.astype(jnp.bfloat16).reshape(-1)
    stack = jnp.concatenate([flat_rows, filtered[:, None]], axis=1)
    gram = lax.psum(
        jnp.einsum("rk,rj->kj", stack, stack, preferred_element_type=jnp.float32), ("gx", "gy")
    )
    gram = gram / total
    lower = jnp.linalg.cholesky(gram)
    solved = lax.linalg.triangular_solve(
        lower, stack.astype(jnp.float32), left_side=False, lower=True, transpose_a=True
    )
    new_modes = solved[:, :modes].astype(jnp.bfloat16).reshape(basis.shape)
    new_mode = solved[:, modes].reshape(basis.shape[:-1])
    return (new_modes, new_mode, lower.T)


def solution(mesh):
    in_specs = (P(None, "gx", "gy", None), P(None, "gx", "gy", None, None), P())
    out_specs = (P(None, "gx", "gy", None, None), P(None, "gx", "gy", None), P())
    return jax.shard_map(local, mesh=mesh, in_specs=in_specs, out_specs=out_specs, check_vma=False)
```

profile of v0, /device:TPU:1, one launch (start us, length us, event | category | flops | bytes accessed | tf_op | source)
XLA Modules:
  0.0 709.4 jit_solution(6518800129823269705)
XLA Ops:
  7.2 0.8 slice_bitcast_fusion.14
  8.3 0.9 fusion.1
  9.2 0.4 convolution_bitcast_fusion
  9.8 4.6 collective-permute-start
  14.4 5.5 collective-permute-start.1
  20.1 0.7 collective-permute-done.1
  21.1 3.1 collective-permute-start.2
  24.1 11.7 %collective-permute-start.3 = (f32[3,8,2,128]{3,2,1,0:T(2,128)S(1)}, f32[3,8,2,128]{3,2,1,0:T(2,128)S(1)}, u32[]{:S(2)}, u32[]{:S(2)}) collective-permute-start(f32[3,8,2,128]{3,2,1,0:T(2,128)S(1)} %convolution_bitcast_fusion.1), channel_id=1, source_target_pairs={{8,0},{16,8},{24,16},{32,24},{40,32},{48,40},{56,48},{64,56},{72,6... | collective-permute-start | bytes 73736 | tf_op jit(solution)/shard_map/ppermute | solution.py:19
  35.9 0.8 collective-permute-done.3
  37.3 1.9 fusion.25
  39.3 1.4 fusion.24
  40.7 462.9 %all-reduce.5.cloned.1.call-done = f32[513,513]{0,1:T(8,128)} async-done(((f32[513,513]{0,1:T(8,128)}), f32[513,513]{0,1:T(8,128)}) %all-reduce.5.cloned.1.call-update) | async-done | bytes 1052692 | tf_op jit(solution)/shard_map/psum | solution.py:50
  503.6 2.5 broadcast_multiply_fusion
  506.1 1.9 copy.56
  508.3 1.0 copy-done.4
  509.3 0.5 cholesky.348
  509.8 11.7 %cholesky.131 = f32[128,128]{1,0:T(8,128)S(1)} custom-call(f32[128,128]{1,0:T(8,128)S(1)} %cholesky.333), custom_call_target="Cholesky" | custom-call | tf_op jit(solution)/shard_map/jit(cholesky)/cholesky | solution.py:54
  521.6 9.8 %custom-call.35 = f32[1,128,128]{1,2,0:T(8,128)S(1)} custom-call(f32[1,128,128]{2,1,0:T(8,128)S(1)} %get-tuple-element.47), custom_call_target="InvertDiagBlocksLowerTriangular" | custom-call | tf_op jit(solution)/shard_map/jit(cholesky)/cholesky | solution.py:54
  531.5 1.4 constant_dynamic-update-slice_fusion.2
  532.9 1.4 convolution_subtract_fusion.3
  534.3 11.9 %cholesky.264 = f32[128,128]{1,0:T(8,128)S(1)} custom-call(f32[128,128]{1,0:T(8,128)S(1)} %cholesky.337), custom_call_target="Cholesky" | custom-call | tf_op jit(solution)/shard_map/jit(cholesky)/cholesky | solution.py:54
  546.2 9.8 %custom-call.36 = f32[1,128,128]{1,2,0:T(8,128)S(1)} custom-call(f32[1,128,128]{2,1,0:T(8,128)S(1)} %get-tuple-element.44), custom_call_target="InvertDiagBlocksLowerTriangular" | custom-call | tf_op jit(solution)/shard_map/jit(cholesky)/cholesky | solution.py:54
  556.0 0.4 convolution_dynamic-update-slice_fusion
  556.4 1.3 convolution_subtract_fusion.4
  557.7 11.7 %cholesky.285 = f32[128,128]{1,0:T(8,128)S(1)} custom-call(f32[128,128]{1,0:T(8,128)S(1)} %cholesky.342), custom_call_target="Cholesky" | custom-call | tf_op jit(solution)/shard_map/jit(cholesky)/cholesky | solution.py:54
  569.5 9.8 %custom-call.37 = f32[1,128,128]{1,2,0:T(8,128)S(1)} custom-call(f32[1,128,128]{2,1,0:T(8,128)S(1)} %get-tuple-element.41), custom_call_target="InvertDiagBlocksLowerTriangular" | custom-call | tf_op jit(solution)/shard_map/jit(cholesky)/cholesky | solution.py:54
  579.5 1.3 convolution_subtract_fusion.5
  580.8 11.9 %cholesky.304 = f32[128,128]{1,0:T(8,128)S(1)} custom-call(f32[128,128]{1,0:T(8,128)S(1)} %cholesky.347), custom_call_target="Cholesky" | custom-call | tf_op jit(solution)/shard_map/jit(cholesky)/cholesky | solution.py:54
  592.8 9.8 %custom-call.38 = f32[1,128,128]{1,2,0:T(8,128)S(1)} custom-call(f32[1,128,128]{2,1,0:T(8,128)S(1)} %get-tuple-element.38), custom_call_target="InvertDiagBlocksLowerTriangular" | custom-call | tf_op jit(solution)/shard_map/jit(cholesky)/cholesky | solution.py:54
  602.9 0.6 multiply_reduce_fusion
  604.9 0.7 compare_reduce_fusion.1
  605.6 0.7 compare_reduce_fusion
  606.3 0.6 compare_reduce_fusion.2
  609.5 1.3 fusion.20
  610.8 0.5 triangular_solve.195
  611.3 10.1 %while.1 = (s32[]{:T(128)}, f32[513,513]{1,0:T(8,128)S(1)}, s32[4,2]{0,1:T(2,128)S(1)}, f32[4,128,128]{2,1,0:T(8,128)}, s32[]{:T(128)}) while((s32[]{:T(128)}, f32[513,513]{1,0:T(8,128)S(1)}, s32[4,2]{0,1:T(2,128)S(1)}, f32[4,128,128]{2,1,0:T(8,128)}, s32[]{:T(128)}) %tuple.44), condition=%wide.while_cond, body=%wide.while_body.sunk | while | flops 2 | bytes 132705 | solution.py:55
  611.3 0.5 fusion.82
  611.9 1.9 bitcast_dynamic-update-slice_fusion.2
  613.9 0.5 fusion.82
  614.4 1.9 bitcast_dynamic-update-slice_fusion.2
  616.4 0.5 fusion.82
  616.9 1.9 bitcast_dynamic-update-slice_fusion.2
  618.9 0.5 fusion.82
  619.4 1.9 bitcast_dynamic-update-slice_fusion.2
  621.4 0.7 fusion.52
  622.1 1.0 pad_maximum_fusion.3
  623.1 49.1 %custom-call.39 = f32[5,128,128]{1,2,0:T(8,128)S(1)} custom-call(f32[5,128,128]{2,1,0:T(8,128)S(1)} %pad_maximum_fusion.3), custom_call_target="InvertDiagBlocksLowerTriangular" | custom-call | tf_op jit(solution)/shard_map/triangular_solve | solution.py:55
  672.2 2.1 bitcast_convert_fusion
  674.3 0.5 triangular_solve.209
  674.8 2.0 convolution_subtract_fusion.1
  676.8 2.1 fusion.73
  678.9 1.2 copy.57
  680.1 2.3 convolution_subtract_fusion.2
  682.4 2.1 fusion.72
  684.5 1.9 copy.59
  686.4 3.1 convolution_subtract_fusion
  689.5 2.1 fusion.71
  691.6 1.9 copy.66
  693.5 2.0 fusion.17
  695.6 0.9 fusion.28
  696.5 0.6 triangular_solve.193
  697.1 1.1 copy.77
  698.2 2.9 copy.69
  701.2 1.0 pad_maximum_fusion.1
  (60 shorter events, 3.0 us)
Async XLA Ops:
  7.2 2.1 copy-start
  7.2 496.4 %all-reduce.5.cloned.1.call-start = ((), (), s32[]{:S(2)}) async-start(), calls=%async_computation | async-start | bytes 2662400 | tf_op jit(solution)/shard_map/psum | solution.py:50
  9.2 28.1 %copy-start.5 = (bf16[3,1,2,128,512]{4,3,2,1,0:T(8,128)(2,1)S(1)}, bf16[3,1,2,128,512]{4,3,2,1,0:T(8,128)(2,1)}, u32[]{:S(2)}) copy-start(bf16[3,1,2,128,512]{4,3,2,1,0:T(8,128)(2,1)} %param.4) | copy-start | bytes 2359300
  9.8 10.3 %collective-permute-start = (f32[3,8,8,128]{3,2,1,0:T(8,128)S(1)}, f32[3,8,8,128]{3,2,1,0:T(8,128)S(1)}, u32[]{:S(2)}, u32[]{:S(2)}) collective-permute-start(f32[3,8,8,128]{3,2,1,0:T(8,128)S(1)} %get-tuple-element.35), channel_id=1, source_target_pairs={{0,1},{1,2},{2,3},{3,4},{4,5},{5,6},{6,7},{8,9},{9,10},{10,11},{11... | collective-permute-start | bytes 294920 | tf_op jit(solution)/shard_map/ppermute | solution.py:16
  14.4 6.4 collective-permute-start.1
  21.1 14.9 %collective-permute-start.2 = (f32[3,8,2,128]{3,2,1,0:T(2,128)S(1)}, f32[3,8,2,128]{3,2,1,0:T(2,128)S(1)}, u32[]{:S(2)}, u32[]{:S(2)}) collective-permute-start(f32[3,8,2,128]{3,2,1,0:T(2,128)S(1)} %convolution_bitcast_fusion.1), channel_id=1, source_target_pairs={{0,8},{8,16},{16,24},{24,32},{32,40},{40,48},{48,56},{56,64},{64,7... | collective-permute-start | bytes 73736 | tf_op jit(solution)/shard_map/ppermute | solution.py:16
  24.1 12.6 %collective-permute-start.3 = (f32[3,8,2,128]{3,2,1,0:T(2,128)S(1)}, f32[3,8,2,128]{3,2,1,0:T(2,128)S(1)}, u32[]{:S(2)}, u32[]{:S(2)}) collective-permute-start(f32[3,8,2,128]{3,2,1,0:T(2,128)S(1)} %convolution_bitcast_fusion.1), channel_id=1, source_target_pairs={{8,0},{16,8},{24,16},{32,24},{40,32},{48,40},{56,48},{64,56},{72,6... | collective-permute-start | bytes 73736 | tf_op jit(solution)/shard_map/ppermute | solution.py:19
  506.1 1.9 copy-start.2
  508.2 1.1 copy-start.4
  621.4 53.5 %copy-start.3 = (f32[513,513]{1,0:T(8,128)}, f32[513,513]{1,0:T(8,128)S(1)}, u32[]{:S(2)}) copy-start(f32[513,513]{1,0:T(8,128)S(1)} %get-tuple-element.109) | copy-start | bytes 3158032
  672.2 2.6 copy-start.9
  674.8 5.2 copy-start.1
  698.2 3.0 copy-start.6
  698.2 2.9 copy-start.7
  698.2 2.9 copy-start.8
Sparse Core Ops, SparseCore 0:
  39.4 464.2 all-reduce.4
where the time goes:
time: 720 us; the launch traced here: 709 us
  waiting for transfers between devices  464 us (64%)
  other arithmetic  149 us (21%)
  matrix products  26.7 us (4%)
  local copies, waits for them, and re-layouts  25.8 us (4%)
  starting transfers between devices  24.9 us (3%)
  between operations  18.8 us (3%)
    psum x1, waiting for transfers between devices, local(): lax.psum(jnp.einsum('rk,rj->kj', stack, stack, preferred_element_type=jnp...  463 us
    another operation x16, other arithmetic, local(): lower = jnp.linalg.cholesky(gram)  89.2 us
    another operation x8, other arithmetic, local(): lax.linalg.triangular_solve(lower, stack.astype(jnp.float32), left_side=F...  52.8 us
    another operation x8, matrix products, local(): lax.linalg.triangular_solve(lower, stack.astype(jnp.float32), left_side=F...  17.8 us
    ppermute x2, starting transfers between devices, padded(): lax.ppermute(lax.slice_in_dim(block, 0, width, axis=dim), axis, backward)  17.2 us
  transfers between devices with their start and end apart: 5, of which 3 were waited for; matrix products, arithmetic and copies ran while one was open for 0% of the time, Pallas kernels for 0%

commit v1 on v0

--- a/solution.py
+++ b/solution.py
@@ -4,6 +4,11 @@
 from jax.sharding import PartitionSpec as P
 
 STRIDE = 8
+
+
+def by_each_axis(x, inner_axis, outer_axis):
+    partial = lax.psum(x, inner_axis)
+    return lax.psum(partial, outer_axis)
 
 
 def padded(block, sides, width, periodic):
@@ -47,8 +52,8 @@
     along_x = jnp.einsum("cxyz,xf->cfyz", padded_x, matrix_x, precision=lax.Precision.HIGHEST)
     filtered = along_x.astype(jnp.bfloat16).reshape(-1)
     stack = jnp.concatenate([flat_rows, filtered[:, None]], axis=1)
-    gram = lax.psum(
-        jnp.einsum("rk,rj->kj", stack, stack, preferred_element_type=jnp.float32), ("gx", "gy")
+    gram = by_each_axis(
+        jnp.einsum("rk,rj->kj", stack, stack, preferred_element_type=jnp.float32), "gx", "gy"
     )
     gram = gram / total
     lower = jnp.linalg.cholesky(gram)

time: 720 us -> 596 us (0.83)
  waiting for transfers between devices: 464 us -> 346 us
    psum x1 -> x2, waiting for transfers between devices: 463 us -> 344 us  [the longest x1 262 us: by_each_axis(): partial = lax.psum(x, inner_axis)]
  transfers between devices with their start and end apart: 5 -> 6, of which waited for: 3 -> 4; matrix products, arithmetic and copies ran while one was open for 0% -> 0% of each run, Pallas kernels for 0% -> 0%
where the time goes in v1:
time: 596 us; the launch traced here: 592 us
  waiting for transfers between devices  346 us (58%)
  other arithmetic  149 us (25%)
  matrix products  26.7 us (4%)
  local copies, waits for them, and re-layouts  26.2 us (4%)
  starting transfers between devices  25.4 us (4%)
  between operations  18.6 us (3%)
    psum x1, waiting for transfers between devices, by_each_axis(): partial = lax.psum(x, inner_axis)  262 us
    another operation x16, other arithmetic, local(): lower = jnp.linalg.cholesky(gram)  89.2 us
    psum x1, waiting for transfers between devices, by_each_axis(): return lax.psum(partial, outer_axis)  82.2 us
    another operation x8, other arithmetic, local(): lax.linalg.triangular_solve(lower, stack.astype(jnp.float32), left_side=F...  52.8 us
    another operation x8, matrix products, local(): lax.linalg.triangular_solve(lower, stack.astype(jnp.float32), left_side=F...  17.8 us
    ppermute x2, starting transfers between devices, padded(): lax.ppermute(lax.slice_in_dim(block, 0, width, axis=dim), axis, backward)  17.2 us
  transfers between devices with their start and end apart: 6, of which 4 were waited for; matrix products, arithmetic and copies ran while one was open for 0% of the time, Pallas kernels for 0%

profile of v1, /device:TPU:1, one launch (start us, length us, event | category | flops | bytes accessed | tf_op | source)
XLA Modules:
  0.0 591.6 jit_solution(2314426309738036667)
XLA Ops:
  7.2 0.8 slice_bitcast_fusion.14
  8.3 0.9 fusion.1
  9.8 4.6 collective-permute-start
  14.4 5.5 collective-permute-start.1
  20.1 0.7 collective-permute-done.1
  21.1 3.1 collective-permute-start.2
  24.1 11.7 %collective-permute-start.3 = (f32[3,8,2,128]{3,2,1,0:T(2,128)S(1)}, f32[3,8,2,128]{3,2,1,0:T(2,128)S(1)}, u32[]{:S(2)}, u32[]{:S(2)}) collective-permute-start(f32[3,8,2,128]{3,2,1,0:T(2,128)S(1)} %convolution_bitcast_fusion.1), channel_id=1, source_target_pairs={{8,0},{16,8},{24,16},{32,24},{40,32},{48,40},{56,48},{64,56},{72,6... | collective-permute-start | bytes 73736 | tf_op jit(solution)/shard_map/ppermute | solution.py:24
  35.9 0.8 collective-permute-done.3
  37.3 1.9 fusion.25
  39.2 0.5 all-reduce.8.cloned.1.call-start
  39.8 262.1 %all-reduce.6.cloned.1.call-done = f32[513,513]{0,1:T(8,128)} async-done(((f32[513,513]{0,1:T(8,128)}), f32[513,513]{0,1:T(8,128)}) %all-reduce.6.cloned.1.call-update) | async-done | bytes 1052692 | tf_op jit(solution)/shard_map/psum | solution.py:10
  301.9 1.4 fusion.24
  303.3 82.2 %all-reduce.8.cloned.1.call-done = f32[513,513]{0,1:T(8,128)} async-done(((f32[513,513]{0,1:T(8,128)}), f32[513,513]{0,1:T(8,128)}) %all-reduce.8.cloned.1.call-update) | async-done | bytes 1052692 | tf_op jit(solution)/shard_map/psum | solution.py:11
  385.5 2.5 broadcast_multiply_fusion
  388.0 1.9 copy.56
  390.2 1.0 copy-done.4
  391.2 0.5 cholesky.348
  391.7 11.7 %cholesky.131 = f32[128,128]{1,0:T(8,128)S(1)} custom-call(f32[128,128]{1,0:T(8,128)S(1)} %cholesky.333), custom_call_target="Cholesky" | custom-call | tf_op jit(solution)/shard_map/jit(cholesky)/cholesky | solution.py:59
  403.5 9.8 %custom-call.35 = f32[1,128,128]{1,2,0:T(8,128)S(1)} custom-call(f32[1,128,128]{2,1,0:T(8,128)S(1)} %get-tuple-element.47), custom_call_target="InvertDiagBlocksLowerTriangular" | custom-call | tf_op jit(solution)/shard_map/jit(cholesky)/cholesky | solution.py:59
  413.4 1.4 constant_dynamic-update-slice_fusion.2
  414.8 1.4 convolution_subtract_fusion.3
  416.2 11.7 %cholesky.264 = f32[128,128]{1,0:T(8,128)S(1)} custom-call(f32[128,128]{1,0:T(8,128)S(1)} %cholesky.337), custom_call_target="Cholesky" | custom-call | tf_op jit(solution)/shard_map/jit(cholesky)/cholesky | solution.py:59
  428.0 9.9 %custom-call.36 = f32[1,128,128]{1,2,0:T(8,128)S(1)} custom-call(f32[1,128,128]{2,1,0:T(8,128)S(1)} %get-tuple-element.44), custom_call_target="InvertDiagBlocksLowerTriangular" | custom-call | tf_op jit(solution)/shard_map/jit(cholesky)/cholesky | solution.py:59
  438.3 1.3 convolution_subtract_fusion.4
  439.6 11.7 %cholesky.285 = f32[128,128]{1,0:T(8,128)S(1)} custom-call(f32[128,128]{1,0:T(8,128)S(1)} %cholesky.342), custom_call_target="Cholesky" | custom-call | tf_op jit(solution)/shard_map/jit(cholesky)/cholesky | solution.py:59
  451.4 9.8 %custom-call.37 = f32[1,128,128]{1,2,0:T(8,128)S(1)} custom-call(f32[1,128,128]{2,1,0:T(8,128)S(1)} %get-tuple-element.41), custom_call_target="InvertDiagBlocksLowerTriangular" | custom-call | tf_op jit(solution)/shard_map/jit(cholesky)/cholesky | solution.py:59
  461.4 1.3 convolution_subtract_fusion.5
  462.7 11.9 %cholesky.304 = f32[128,128]{1,0:T(8,128)S(1)} custom-call(f32[128,128]{1,0:T(8,128)S(1)} %cholesky.347), custom_call_target="Cholesky" | custom-call | tf_op jit(solution)/shard_map/jit(cholesky)/cholesky | solution.py:59
  474.7 9.8 %custom-call.38 = f32[1,128,128]{1,2,0:T(8,128)S(1)} custom-call(f32[1,128,128]{2,1,0:T(8,128)S(1)} %get-tuple-element.38), custom_call_target="InvertDiagBlocksLowerTriangular" | custom-call | tf_op jit(solution)/shard_map/jit(cholesky)/cholesky | solution.py:59
  484.8 0.6 multiply_reduce_fusion
  486.9 0.7 compare_reduce_fusion.1
  487.5 0.7 compare_reduce_fusion
  488.2 0.6 compare_reduce_fusion.2
  491.4 1.3 fusion.20
  492.7 0.5 triangular_solve.195
  493.2 10.6 %while.1 = (s32[]{:T(128)}, f32[513,513]{1,0:T(8,128)S(1)}, s32[4,2]{0,1:T(2,128)S(1)}, f32[4,128,128]{2,1,0:T(8,128)}, s32[]{:T(128)}) while((s32[]{:T(128)}, f32[513,513]{1,0:T(8,128)S(1)}, s32[4,2]{0,1:T(2,128)S(1)}, f32[4,128,128]{2,1,0:T(8,128)}, s32[]{:T(128)}) %tuple.44), condition=%wide.while_cond, body=%wide.while_body.sunk | while | flops 2 | bytes 132705 | solution.py:60
  493.2 0.6 fusion.82
  493.8 2.0 bitcast_dynamic-update-slice_fusion.2
  495.9 0.6 fusion.82
  496.5 2.0 bitcast_dynamic-update-slice_fusion.2
  498.5 0.6 fusion.82
  499.1 2.0 bitcast_dynamic-update-slice_fusion.2
  501.2 0.6 fusion.82
  501.7 2.0 bitcast_dynamic-update-slice_fusion.2
  503.7 0.7 fusion.52
  504.5 1.0 pad_maximum_fusion.3
  505.4 49.1 %custom-call.39 = f32[5,128,128]{1,2,0:T(8,128)S(1)} custom-call(f32[5,128,128]{2,1,0:T(8,128)S(1)} %pad_maximum_fusion.3), custom_call_target="InvertDiagBlocksLowerTriangular" | custom-call | tf_op jit(solution)/shard_map/triangular_solve | solution.py:60
  554.6 2.1 bitcast_convert_fusion
  556.7 0.5 triangular_solve.209
  557.2 2.0 convolution_subtract_fusion.1
  559.2 2.1 fusion.73
  561.3 1.2 copy.57
  562.5 2.3 convolution_subtract_fusion.2
  564.8 2.1 fusion.72
  566.9 1.9 copy.59
  568.8 3.1 convolution_subtract_fusion
  571.9 2.1 fusion.71
  574.0 1.9 copy.66
  575.9 2.0 fusion.17
  578.0 0.9 fusion.28
  578.9 0.6 triangular_solve.193
  579.5 1.1 copy.77
  580.6 2.9 copy.69
  583.5 1.0 pad_maximum_fusion.1
  (63 shorter events, 3.8 us)
Async XLA Ops:
  7.2 2.1 copy-start
  7.2 294.6 %all-reduce.6.cloned.1.call-start = ((), (), s32[]{:S(2)}) async-start(), calls=%async_computation | async-start | bytes 2662400 | tf_op jit(solution)/shard_map/psum | solution.py:10
  9.2 28.1 %copy-start.5 = (bf16[3,1,2,128,512]{4,3,2,1,0:T(8,128)(2,1)S(1)}, bf16[3,1,2,128,512]{4,3,2,1,0:T(8,128)(2,1)}, u32[]{:S(2)}) copy-start(bf16[3,1,2,128,512]{4,3,2,1,0:T(8,128)(2,1)} %param.4) | copy-start | bytes 2359300
  9.8 10.3 %collective-permute-start = (f32[3,8,8,128]{3,2,1,0:T(8,128)S(1)}, f32[3,8,8,128]{3,2,1,0:T(8,128)S(1)}, u32[]{:S(2)}, u32[]{:S(2)}) collective-permute-start(f32[3,8,8,128]{3,2,1,0:T(8,128)S(1)} %get-tuple-element.35), channel_id=1, source_target_pairs={{0,1},{1,2},{2,3},{3,4},{4,5},{5,6},{6,7},{8,9},{9,10},{10,11},{11... | collective-permute-start | bytes 294920 | tf_op jit(solution)/shard_map/ppermute | solution.py:21
  14.4 6.4 %collective-permute-start.1 = (f32[3,8,8,128]{3,2,1,0:T(8,128)S(1)}, f32[3,8,8,128]{3,2,1,0:T(8,128)S(1)}, u32[]{:S(2)}, u32[]{:S(2)}) collective-permute-start(f32[3,8,8,128]{3,2,1,0:T(8,128)S(1)} %get-tuple-element.36), channel_id=1, source_target_pairs={{1,0},{2,1},{3,2},{4,3},{5,4},{6,5},{7,6},{9,8},{10,9},{11,10},{12... | collective-permute-start | bytes 294920 | tf_op jit(solution)/shard_map/ppermute | solution.py:24
  21.1 14.9 %collective-permute-start.2 = (f32[3,8,2,128]{3,2,1,0:T(2,128)S(1)}, f32[3,8,2,128]{3,2,1,0:T(2,128)S(1)}, u32[]{:S(2)}, u32[]{:S(2)}) collective-permute-start(f32[3,8,2,128]{3,2,1,0:T(2,128)S(1)} %convolution_bitcast_fusion.1), channel_id=1, source_target_pairs={{0,8},{8,16},{16,24},{24,32},{32,40},{40,48},{48,56},{56,64},{64,7... | collective-permute-start | bytes 73736 | tf_op jit(solution)/shard_map/ppermute | solution.py:21
  24.1 12.6 %collective-permute-start.3 = (f32[3,8,2,128]{3,2,1,0:T(2,128)S(1)}, f32[3,8,2,128]{3,2,1,0:T(2,128)S(1)}, u32[]{:S(2)}, u32[]{:S(2)}) collective-permute-start(f32[3,8,2,128]{3,2,1,0:T(2,128)S(1)} %convolution_bitcast_fusion.1), channel_id=1, source_target_pairs={{8,0},{16,8},{24,16},{32,24},{40,32},{48,40},{56,48},{64,56},{72,6... | collective-permute-start | bytes 73736 | tf_op jit(solution)/shard_map/ppermute | solution.py:24
  39.2 346.3 %all-reduce.8.cloned.1.call-start = ((), (), s32[]{:S(2)}) async-start(), calls=%async_computation.1 | async-start | bytes 2662400 | tf_op jit(solution)/shard_map/psum | solution.py:11
  388.0 1.9 copy-start.2
  390.1 1.1 copy-start.4
  503.7 53.5 %copy-start.3 = (f32[513,513]{1,0:T(8,128)}, f32[513,513]{1,0:T(8,128)S(1)}, u32[]{:S(2)}) copy-start(f32[513,513]{1,0:T(8,128)S(1)} %get-tuple-element.110) | copy-start | bytes 3158032
  554.6 2.6 copy-start.9
  557.2 5.2 copy-start.1
  580.6 3.0 copy-start.6
  580.6 2.9 copy-start.7
  580.6 2.9 copy-start.8
Sparse Core Ops, SparseCore 0:
  39.4 262.4 all-reduce.5
  304.2 81.2 all-reduce.7
